TPU v7x, 32 devices: a whole 2x2x4 slice. The times are simulated.
32 devices in a mesh: frames: 8 (over y, x, core), heads: 4 (over z).
Axes of the slice: x: 2, y: 2, z: 4, core: 2. Of those that a mesh axis runs over, the one named last changes fastest.
Arguments:
- frames: bfloat16 [8192, 1152], P('frames', 'heads'), may hold values from -6 to 6
- latents: bfloat16 [256, 1152], P('frames'), may hold values from -400 to 400
- w_query: bfloat16 [1152, 4096], P(None, 'heads'), may hold values from -0.1875 to 0.1875
- w_key: bfloat16 [1152, 4096], P(None, 'heads'), may hold values from -0.1875 to 0.1875
- w_value: bfloat16 [1152, 4096], P(None, 'heads'), may hold values from -0.1875 to 0.1875
- w_out: bfloat16 [4096, 8192], P('heads', 'frames'), may hold values from -0.09375 to 0.09375
- norm_gain: float32 [8192], P('frames'), may hold values from 0.5 to 1.5
- w_gate: bfloat16 [8192, 16384], P('frames', 'heads'), may hold values from -0.0625 to 0.0625
- w_up: bfloat16 [8192, 16384], P('frames', 'heads'), may hold values from -0.0625 to 0.0625
- w_down: bfloat16 [16384, 8192], P('heads', 'frames'), may hold values from -0.046875 to 0.046875
Outputs:
- block_out: bfloat16 [256, 8192], P('heads', 'frames')
All inputs are finite; a program needn't handle non-finite values.
Results may differ from a plain program's by a relative error of at most 0.023.
Values may be sent and summed in bfloat16 or wider, within the bound.
A program may use at most 128 MiB of HBM per device.

v0:
```python
import jax
import jax.numpy as jnp
from jax import lax
from jax.sharding import PartitionSpec as P

HDIM = 128
D = 8192


norm_eps = 1e-06


def on_device(frames, latents, w_query, w_key, w_value, w_out, norm_gain, w_gate, w_up, w_down):
    local_query = jnp.dot(latents, w_query, preferred_element_type=jnp.float32).astype(jnp.bfloat16)
    queries = lax.all_gather(local_query, "frames", axis=0, tiled=True)
    width = w_key.shape[1]
    piece = lax.all_gather(frames, "heads", axis=1, tiled=True)
    keys = jnp.dot(piece, w_key, preferred_element_type=jnp.float32)
    values = jnp.dot(piece, w_value, preferred_element_type=jnp.float32)
    heads_here = width // HDIM
    latent_count = queries.shape[0]
    query_heads = queries.reshape(latent_count, heads_here, HDIM)
    key_heads = keys.astype(jnp.bfloat16).reshape(-1, heads_here, HDIM)
    value_heads = values.astype(jnp.bfloat16).reshape(-1, heads_here, HDIM)
    scores = jnp.einsum(
        "qhd,khd->qhk", query_heads, key_heads, preferred_element_type=jnp.float32
    ) * HDIM ** (-0.5)
    local_max = jnp.max(scores, axis=2)
    score_peak = lax.pmax(local_max, "frames")
    weights = jnp.exp(scores - score_peak[:, :, None])
    total = jnp.sum(weights, axis=2)
    mixed = jnp.einsum(
        "qhk,khd->qhd",
        weights.astype(jnp.bfloat16),
        value_heads,
        preferred_element_type=jnp.float32,
    )
    total, mixed = (total, mixed)
    total_all, mixed_all = lax.psum((total, mixed), "frames")
    attention = (
        (mixed_all / total_all[:, :, None]).reshape(latent_count, width).astype(jnp.bfloat16)
    )
    latent_state = lax.psum_scatter(
        jnp.dot(attention, w_out, preferred_element_type=jnp.float32),
        "heads",
        scatter_dimension=0,
        tiled=True,
    ).astype(jnp.bfloat16)
    latent_full = lax.all_gather(latent_state, "heads", axis=0, tiled=True)
    full_float = latent_full.astype(jnp.float32)
    square_part = jnp.sum(full_float * full_float, axis=1)
    normed = (full_float * norm_gain[None, :]).astype(jnp.bfloat16)
    gate_part = jnp.dot(normed, w_gate, preferred_element_type=jnp.float32)
    up_part = jnp.dot(normed, w_up, preferred_element_type=jnp.float32)
    squares = lax.psum(square_part, "frames")
    gate_sum, up_sum = (
        lax.psum_scatter(gate_part, "frames", scatter_dimension=0, tiled=True),
        lax.psum_scatter(up_part, "frames", scatter_dimension=0, tiled=True),
    )
    share_rows = gate_sum.shape[0]
    square_rows = lax.dynamic_slice_in_dim(
        squares, lax.axis_index("frames") * share_rows, share_rows, 0
    )
    scale_rows = lax.rsqrt(square_rows / D + norm_eps)[:, None]
    hidden = (jax.nn.silu(gate_sum * scale_rows) * (up_sum * scale_rows)).astype(jnp.bfloat16)
    hidden_full = lax.all_gather(hidden, "frames", axis=0, tiled=True)
    down = lax.psum_scatter(
        jnp.dot(hidden_full, w_down, preferred_element_type=jnp.float32),
        "heads",
        scatter_dimension=0,
        tiled=True,
    )
    return (latent_state.astype(jnp.float32) + down).astype(jnp.bfloat16)


def solution(mesh):
    placed = (
        P("frames", "heads"),
        P("frames", None),
        P(None, "heads"),
        P(None, "heads"),
        P(None, "heads"),
        P("heads", "frames"),
        P("frames"),
        P("frames", "heads"),
        P("frames", "heads"),
        P("heads", "frames"),
    )
    return jax.shard_map(
        on_device, mesh=mesh, in_specs=placed, out_specs=P("heads", "frames"), check_vma=False
    )
```

profile of v0, /device:TPU:24, one launch (start us, length us, event | category | flops | bytes accessed | tf_op | source)
XLA Modules:
  0.0 377.1 jit_solution(17033248444344372530)
XLA Ops:
  7.3 2.2 convolution_convert_fusion.2
  9.5 9.9 %all_gather.13 = bf16[256,1024]{1,0:T(8,128)(2,1)S(1)} all-gather(bf16[32,1024]{1,0:T(8,128)(2,1)S(1)} %convolution_convert_fusion.2), channel_id=1, replica_groups=mesh['frames'=8,'heads'=4] {'frames'}, dimensions={0}, use_global_device_ids=true | all-gather | bytes 589824 | tf_op jit(solution)/shard_map/all_gather | solution.py:15
  19.4 38.6 %all-gather.3.cloned.1.call-done = bf16[1024,1152]{0,1:T(8,128)(2,1)} async-done(((bf16[1024,288]{0,1:T(8,128)(2,1)}), bf16[1024,1152]{0,1:T(8,128)(2,1)}) %all-gather.3.cloned.1.call-update) | async-done | bytes 2359312 | tf_op jit(solution)/shard_map/all_gather | solution.py:17
  58.0 4.8 %convolution_convert_fusion = bf16[1024,1024]{0,1:T(8,128)(2,1)S(1)} fusion(bf16[1024,1152]{0,1:T(8,128)(2,1)} %all-gather.3.cloned.1.call-done, bf16[1152,1024]{1,0:T(8,128)(2,1)S(1)} %copy-done), kind=kOutput, calls=%fused_computation.8 | convolution fusion | flops 2416967680 | bytes 6815744 | tf_op jit(solution)/shard_map/dot_general | solution.py:18
  62.8 4.5 %bitcast_reduce_fusion = (f32[256,8]{0,1:T(8,128)S(1)}, f32[8,1024,256]{2,1,0:T(8,128)}) fusion(bf16[1024,8,128]{0,2,1:T(8,128)(2,1)S(1)} %bitcast.42, bf16[256,1024]{1,0:T(8,128)(2,1)S(1)} %all_gather.13), kind=kOutput, calls=%fused_computation.1 | convolution fusion | flops 541063168 | bytes 11018240 | tf_op jit(solution)/shard_map/qhd,khd->qhk/dot_general | solution.py:25
  67.3 14.3 %pmax.7 = f32[256,8]{0,1:T(8,128)S(1)} all-reduce(f32[256,8]{0,1:T(8,128)S(1)} %get-tuple-element.5), channel_id=1, replica_groups=mesh['frames'=8,'heads'=4] {'frames'}, use_global_device_ids=true, to_apply=%region_1.0 | all-reduce | flops 2048 | bytes 16384 | tf_op jit(solution)/shard_map/pmax | solution.py:29
  81.6 5.5 %convolution_convert_fusion.1 = bf16[1024,1024]{0,1:T(8,128)(2,1)S(1)} fusion(bf16[1024,1152]{0,1:T(8,128)(2,1)} %all-gather.3.cloned.1.call-done, bf16[1152,1024]{1,0:T(8,128)(2,1)} %param.14), kind=kOutput, calls=%fused_computation.9 | convolution fusion | flops 2416967680 | bytes 6815744 | tf_op jit(solution)/shard_map/dot_general | solution.py:19
  87.1 2.5 fusion.7
  89.7 4.8 %fusion.1 = f32[256,8]{0,1:T(8,128)S(1)} fusion(f32[8,1024,256]{2,1,0:T(8,128)} %get-tuple-element.6, f32[256,8]{0,1:T(8,128)S(1)} %pmax.7), kind=kLoop, calls=%fused_computation.3 | loop fusion | flops 6289408 | bytes 8404992 | tf_op jit(solution)/shard_map/reduce_sum | solution.py:31
  94.4 12.2 %psum.22 = f32[256,8]{0,1:T(8,128)S(1)} all-reduce(f32[256,8]{0,1:T(8,128)S(1)} %fusion.1), channel_id=1, replica_groups=mesh['frames'=8,'heads'=4] {'frames'}, use_global_device_ids=true, to_apply=%region_4.0 | all-reduce | flops 2048 | bytes 16384 | tf_op jit(solution)/shard_map/psum | solution.py:39
  106.6 38.9 %all-reduce.2.cloned.1.call-done = f32[256,8,128]{0,2,1:T(8,128)} async-done(((f32[256,8,128]{0,2,1:T(8,128)}), f32[256,8,128]{0,2,1:T(8,128)}) %all-reduce.2.cloned.1.call-update) | async-done | bytes 1048592 | tf_op jit(solution)/shard_map/psum | solution.py:39
  146.8 3.3 fusion.20
  150.2 24.1 %reduce-scatter.5.cloned.1.call-done = f32[64,1024]{1,0:T(8,128)} async-done(((f32[256,1024]{1,0:T(8,128)}), f32[64,1024]{1,0:T(8,128)}) %reduce-scatter.5.cloned.1.call-update) | async-done | bytes 262160 | tf_op jit(solution)/shard_map/reduce_scatter | solution.py:43
  175.3 15.5 %all_gather.14 = bf16[256,1024]{1,0:T(8,128)(2,1)S(1)} all-gather(bf16[64,1024]{1,0:T(8,128)(2,1)S(1)} %convert_element_type.42), channel_id=1, replica_groups=mesh['frames'=8,'heads'=4] {'heads'}, dimensions={0}, use_global_device_ids=true | all-gather | bytes 655360 | tf_op jit(solution)/shard_map/all_gather | solution.py:49
  190.8 7.6 %fusion.15 = f32[256,4096]{1,0:T(8,128)} fusion(bf16[1024,4096]{1,0:T(8,128)(2,1)} %param.18, bf16[256,1024]{1,0:T(8,128)(2,1)S(1)} %all_gather.14, f32[1024]{0:T(1024)S(1)} %copy-done.4), kind=kOutput, calls=%fused_computation.21 | convolution fusion | flops 2148270080 | bytes 13111296 | tf_op jit(solution)/shard_map/dot_general | solution.py:54
  198.5 7.7 %fusion.17 = f32[256,4096]{1,0:T(8,128)} fusion(bf16[1024,4096]{1,0:T(8,128)(2,1)} %param.17, bf16[256,1024]{1,0:T(8,128)(2,1)S(1)} %all_gather.14, f32[1024]{0:T(1024)S(1)} %copy-done.4), kind=kOutput, calls=%fused_computation.22 | convolution fusion | flops 2148270080 | bytes 13111296 | tf_op jit(solution)/shard_map/dot_general | solution.py:53
  206.5 11.8 %psum.23 = f32[256]{0:T(256)S(1)} all-reduce(f32[256]{0:T(256)S(1)} %fusion.11), channel_id=1, replica_groups=mesh['frames'=8,'heads'=4] {'frames'}, use_global_device_ids=true, to_apply=%region_8.0 | all-reduce | flops 256 | bytes 2048 | tf_op jit(solution)/shard_map/psum | solution.py:55
  218.4 33.0 %reduce-scatter.9.cloned.1.call-done = f32[32,4096]{1,0:T(8,128)} async-done(((f32[256,4096]{1,0:T(8,128)}), f32[32,4096]{1,0:T(8,128)}) %reduce-scatter.9.cloned.1.call-update) | async-done | bytes 524304 | tf_op jit(solution)/shard_map/reduce_scatter | solution.py:58
  251.3 54.6 %reduce-scatter.7.cloned.1.call-done = f32[32,4096]{1,0:T(8,128)} async-done(((f32[256,4096]{1,0:T(8,128)}), f32[32,4096]{1,0:T(8,128)}) %reduce-scatter.7.cloned.1.call-update) | async-done | bytes 524304 | tf_op jit(solution)/shard_map/reduce_scatter | solution.py:57
  305.9 2.1 multiply_convert_fusion
  308.1 28.0 %all-gather.5.cloned.1.call-done = bf16[256,4096]{1,0:T(8,128)(2,1)} async-done(((bf16[32,4096]{1,0:T(8,128)(2,1)}), bf16[256,4096]{1,0:T(8,128)(2,1)}) %all-gather.5.cloned.1.call-update) | async-done | bytes 2097168 | tf_op jit(solution)/shard_map/all_gather | solution.py:66
  336.1 7.5 %fusion.21 = f32[256,1024]{1,0:T(8,128)} fusion(bf16[256,4096]{1,0:T(8,128)(2,1)} %all-gather.5.cloned.1.call-done, bf16[4096,1024]{1,0:T(8,128)(2,1)} %param.19), kind=kOutput, calls=%fused_computation.27 | convolution fusion | flops 2147483648 | bytes 11534336 | tf_op jit(solution)/shard_map/dot_general | solution.py:68
  343.6 25.0 %reduce-scatter.11.cloned.1.call-done = f32[64,1024]{1,0:T(8,128)} async-done(((f32[256,1024]{1,0:T(8,128)}), f32[64,1024]{1,0:T(8,128)}) %reduce-scatter.11.cloned.1.call-update) | async-done | bytes 262160 | tf_op jit(solution)/shard_map/reduce_scatter | solution.py:67
  368.6 1.6 add_convert_fusion
  (28 shorter events, 3.6 us)
Async XLA Ops:
  6.5 51.4 %copy-start = (bf16[1152,1024]{1,0:T(8,128)(2,1)S(1)}, bf16[1152,1024]{1,0:T(8,128)(2,1)}, u32[]{:S(2)}) copy-start(bf16[1152,1024]{1,0:T(8,128)(2,1)} %param.13) | copy-start | bytes 7077892
  6.5 51.4 %all-gather.3.cloned.1.call-start = ((), (), s32[]{:S(2)}) async-start(), calls=%async_computation.4 | async-start | bytes 2949120 | tf_op jit(solution)/shard_map/all_gather | solution.py:17
  7.3 138.2 %all-reduce.2.cloned.1.call-start = ((), (), s32[]{:S(2)}) async-start(), calls=%async_computation.5 | async-start | bytes 2097152 | tf_op jit(solution)/shard_map/psum | solution.py:39
  81.6 5.5 %copy-start.2 = (f32[8,1024,256]{2,1,0:T(8,128)S(1)}, f32[8,1024,256]{2,1,0:T(8,128)}, u32[]{:S(2)}) copy-start(f32[8,1024,256]{2,1,0:T(8,128)} %get-tuple-element.6) | copy-start | bytes 25165828
  89.6 84.7 %reduce-scatter.5.cloned.1.call-start = ((), (), s32[]{:S(2)}) async-start(), calls=%async_computation.6 | async-start | bytes 1310720 | tf_op jit(solution)/shard_map/reduce_scatter | solution.py:43
  94.4 96.4 %copy-start.4 = (f32[1024]{0:T(1024)S(1)}, f32[1024]{0:T(1024)}, u32[]{:S(2)}) copy-start(f32[1024]{0:T(1024)} %param.16) | copy-start | bytes 12292
  150.1 101.2 %reduce-scatter.9.cloned.1.call-start = ((), (), s32[]{:S(2)}) async-start(), calls=%async_computation.8 | async-start | bytes 4718592 | tf_op jit(solution)/shard_map/reduce_scatter | solution.py:58
  198.5 107.4 %reduce-scatter.7.cloned.1.call-start = ((), (), s32[]{:S(2)}) async-start(), calls=%async_computation.7 | async-start | bytes 4718592 | tf_op jit(solution)/shard_map/reduce_scatter | solution.py:57
  206.2 129.9 %all-gather.5.cloned.1.call-start = ((), (), s32[]{:S(2)}) async-start(), calls=%async_computation.9 | async-start | bytes 2359296 | tf_op jit(solution)/shard_map/all_gather | solution.py:66
  308.1 60.5 %copy-start.3 = (f32[64,1024]{1,0:T(8,128)S(1)}, f32[64,1024]{1,0:T(8,128)}, u32[]{:S(2)}) copy-start(f32[64,1024]{1,0:T(8,128)} %reduce-scatter.5.cloned.1.call-done) | copy-start | bytes 786436
  308.1 60.5 %reduce-scatter.11.cloned.1.call-start = ((), (), s32[]{:S(2)}) async-start(), calls=%async_computation.10 | async-start | bytes 1310720 | tf_op jit(solution)/shard_map/reduce_scatter | solution.py:67
  336.1 34.1 %copy-start.1 = (bf16[1152,1024]{1,0:T(8,128)(2,1)S(1)}, bf16[1152,1024]{1,0:T(8,128)(2,1)}, u32[]{:S(2)}) copy-start(bf16[1152,1024]{1,0:T(8,128)(2,1)} %param.13) | copy-start | bytes 7077892
Sparse Core Ops, SparseCore 0:
  8.9 48.9 all-gather.2
  89.7 55.7 all-reduce.1
  150.3 24.0 reduce-scatter.4
  198.6 52.6 reduce-scatter.8
  254.5 51.3 reduce-scatter.6
  308.2 27.8 all-gather.4
  343.7 24.8 reduce-scatter.10
where the time goes:
time: 382 us; the launch traced here: 377 us
  waiting for transfers between devices  243 us (64%)
  blocking collectives  63.6 us (17%)
  matrix products  45.6 us (12%)
  between operations  13.6 us (4%)
  other arithmetic  11.1 us (3%)
    reduce_scatter x1, waiting for transfers between devices, on_device(): lax.psum_scatter(gate_part, 'frames', scatter_dimension=0, tiled=True)  54.6 us
    psum x1, waiting for transfers between devices, on_device(): total_all, mixed_all = lax.psum((total, mixed), 'frames')  38.9 us
    all_gather x1, waiting for transfers between devices, on_device(): piece = lax.all_gather(frames, 'heads', axis=1, tiled=True)  38.6 us
    reduce_scatter x1, waiting for transfers between devices, on_device(): lax.psum_scatter(up_part, 'frames', scatter_dimension=0, tiled=True)  33 us
    all_gather x1, waiting for transfers between devices, on_device(): hidden_full = lax.all_gather(hidden, 'frames', axis=0, tiled=True)  28 us
    reduce_scatter x1, waiting for transfers between devices, on_device(): lax.psum_scatter(jnp.dot(hidden_full, w_down, preferred_element_type=jnp....  25 us
    reduce_scatter x1, waiting for transfers between devices, on_device(): lax.psum_scatter(jnp.dot(attention, w_out, preferred_element_type=jnp.flo...  24.1 us
    all_gather x1, blocking collectives, on_device(): latent_full = lax.all_gather(latent_state, 'heads', axis=0, tiled=True)  15.5 us
  transfers between devices with their start and end apart: 7, of which 7 were waited for; matrix products, arithmetic and copies ran while one was open for 4% of the time, Pallas kernels for 0%

commit v1 on v0

v1 whole, which is shorter than its diff:
```python
import math

import jax
import jax.numpy as jnp
from jax import lax
from jax.experimental import pallas as pl
from jax.experimental.pallas import tpu as pltpu
from jax.sharding import PartitionSpec as P

HDIM = 128
norm_eps = 1e-06
F32 = jnp.float32
BF16 = jnp.bfloat16
MIB = 2**20


def rcopy(src, dst, ssem, rsem, axis, peer):
    return pltpu.make_async_remote_copy(
        src_ref=src,
        dst_ref=dst,
        send_sem=ssem,
        recv_sem=rsem,
        device_id={axis: peer},
        device_id_type=pl.DeviceIdType.MESH,
    )


def loop(lo, hi, body):
    def step(i, carry):
        body(i)
        return carry

    lax.fori_loop(lo, hi, step, 0)


def flat(value):
    rows, cols = value.shape[-2], value.shape[-1]
    if rows % 16:
        return value.astype(F32).reshape(-1, cols).astype(value.dtype)
    return value.reshape(-1, cols)


def tile_of(size, want):
    return want if size % want == 0 else size


def attend_kernel(
    nf, nh,
    fr, lat, wq, wk, wv,
    mix_out, stat_out,
    fr_all, q_all, wq_v, wkv, acc,
    w_sem, rs_sem, ls_sem, fr_sem, qs_sem, qr_sem,
):
    me = lax.axis_index("frames")
    hz = lax.axis_index("heads")
    width = wq.shape[1]
    heads = width // HDIM
    tokens = fr.shape[0]

    c_q = pltpu.make_async_copy(wq, wq_v, w_sem.at[0])
    c_k = pltpu.make_async_copy(wk, wkv.at[0], w_sem.at[1])
    c_v = pltpu.make_async_copy(wv, wkv.at[1], w_sem.at[2])
    c_q.start()
    c_k.start()
    c_v.start()

    barrier = pltpu.get_barrier_semaphore()

    def greet(d):
        pl.semaphore_signal(
            barrier, inc=1, device_id={"frames": lax.rem(me + d, nf)},
            device_id_type=pl.DeviceIdType.MESH)

    loop(1, nf, greet)
    has_l = hz > 0
    has_r = hz < nh - 1

    @pl.when(has_l)
    def _():
        pl.semaphore_signal(barrier, inc=1, device_id={"heads": hz - 1},
                            device_id_type=pl.DeviceIdType.MESH)

    @pl.when(has_r)
    def _():
        pl.semaphore_signal(barrier, inc=1, device_id={"heads": hz + 1},
                            device_id_type=pl.DeviceIdType.MESH)

    pl.semaphore_wait(barrier, nf - 1 + has_l.astype(jnp.int32) + has_r.astype(jnp.int32))

    def right(s, src, b):
        return rcopy(src, fr_all.at[b], rs_sem.at[s], fr_sem.at[b], "heads", hz + 1)

    def left(s, src, b):
        return rcopy(src, fr_all.at[b], ls_sem.at[s], fr_sem.at[b], "heads", hz - 1)

    @pl.when(has_r)
    def _():
        right(0, fr, hz).start()

    @pl.when(has_l)
    def _():
        left(0, fr, hz).start()

    c_q.wait()
    q_all[me] = jnp.dot(lat[...], wq_v[...], preferred_element_type=F32).astype(BF16)

    def qcopy(d):
        return rcopy(q_all.at[me], q_all.at[me], qs_sem.at[d], qr_sem.at[d],
                     "frames", lax.rem(me + d, nf))

    loop(1, nf, lambda d: qcopy(d).start())
    c_k.wait()
    c_v.wait()

    tt = tile_of(tokens, 256)

    def project(x, b, first):
        def tile(i):
            rows = pl.ds(pl.multiple_of(i * tt, tt), tt)
            xb = x[rows, :]
            for w in range(2):
                term = jnp.dot(xb, wkv[w, b], preferred_element_type=F32)
                if first:
                    acc[w, rows, :] = term
                else:
                    acc[w, rows, :] += term
        loop(0, tokens // tt, tile)

    project(fr, hz, True)

    def hop(s):
        lb, rb = hz - s, hz + s

        @pl.when(lb >= 0)
        def _():
            right(s, fr, lb).wait_recv()

            @pl.when(has_r)
            def _():
                right(s, fr_all.at[lb], lb).start()

        @pl.when(rb < nh)
        def _():
            right(s, fr, rb).wait_recv()

            @pl.when(has_l)
            def _():
                left(s, fr_all.at[rb], rb).start()

        @pl.when(lb >= 0)
        def _():
            project(fr_all.at[lb], lb, False)

        @pl.when(rb < nh)
        def _():
            project(fr_all.at[rb], rb, False)

    loop(1, nh, hop)
    loop(1, nf, lambda d: qcopy(d).wait_recv())

    scale = HDIM ** (-0.5)
    latents = mix_out.shape[0]
    lane = lax.broadcasted_iota(jnp.int32, (latents, 128), 1)
    peaks = jnp.zeros((latents, 128), F32)
    sums = jnp.ones((latents, 128), F32)
    for h in range(heads):
        cols = slice(h * HDIM, (h + 1) * HDIM)
        q = flat(q_all[:, :, cols])
        k = acc[0, :, cols].astype(BF16)
        v = acc[1, :, cols].astype(BF16)
        scores = lax.dot_general(q, k, (((1,), (1,)), ((), ())),
                                 preferred_element_type=F32) * scale
        peak = jnp.max(scores, axis=1, keepdims=True)
        weights = jnp.exp(scores - peak)
        total = jnp.sum(weights, axis=1, keepdims=True)
        mixed = jnp.dot(weights.astype(BF16), v, preferred_element_type=F32)
        mix_out[:, cols] = (mixed / total).astype(BF16)
        peaks = jnp.where(lane == h, peak, peaks)
        sums = jnp.where(lane == h, total, sums)
    stat_out[:, :128] = peaks
    stat_out[:, 128:] = sums

    loop(1, nf, lambda d: qcopy(d).wait_send())

    def drain(s):
        @pl.when((hz - s >= 0) & has_r)
        def _():
            right(s, fr, hz).wait_send()

        @pl.when((hz + s < nh) & has_l)
        def _():
            left(s, fr, hz).wait_send()

    loop(0, nh, drain)


def block_kernel(
    nf, nh, ny, nx,
    mix, stat, gain, w_out, w_gate, w_up, w_down,
    out,
    wo, wg, wu, wd,
    rm, rst, att_all, part, rz, lat_all, nrm, sqp, rsq,
    gu, rc, r2a, r2b, s2a, s2b, r3a, r3b, hid, dp, rd,
    w_sem, mix_s, mix_r, st_s, st_r, at_s, at_r, z_s, z_r, l_s, l_r, sq_s, sq_r,
    c_s, c_r, x2_s, x2_r, y2_s, y2_r, x3_s, x3_r, y3_s, y3_r,
    hy_s, hy_r, hx_s, hx_r, gx_s, gx_r, gy_s, gy_r, hc_s, hc_r, d_s, d_r,
):
    me = lax.axis_index("frames")
    hz = lax.axis_index("heads")
    core = lax.rem(me, 2)
    xi = lax.rem(me // 2, nx)
    yi = me // (2 * nx)
    r, width = mix.shape[1], mix.shape[2]
    heads = width // HDIM
    fh = nf // nh
    cols_d = wo.shape[1]
    units = wg.shape[1]
    half = units // 2
    latents = nf * r

    copies = [
        pltpu.make_async_copy(src, dst, w_sem.at[i])
        for i, (src, dst) in enumerate(
            [(w_out, wo), (w_gate, wg), (w_up, wu), (w_down, wd)])
    ]
    for c in copies:
        c.start()

    barrier = pltpu.get_barrier_semaphore()

    def fpeer(d):
        return lax.rem(me + d, nf)

    def zpeer(d):
        return lax.rem(hz + d, nh)

    def xpeer(d):
        return lax.rem(xi + d, nx)

    def ypeer(d):
        return lax.rem(yi + d, ny)

    def xdev(x):
        return (yi * nx + x) * 2 + core

    def ydev(y):
        return (y * nx + xi) * 2 + core

    def greet_f(d):
        pl.semaphore_signal(barrier, inc=1, device_id={"frames": fpeer(d)},
                            device_id_type=pl.DeviceIdType.MESH)

    def greet_z(d):
        pl.semaphore_signal(barrier, inc=1, device_id={"heads": zpeer(d)},
                            device_id_type=pl.DeviceIdType.MESH)

    loop(1, nf, greet_f)
    loop(1, nh, greet_z)
    pl.semaphore_wait(barrier, nf + nh - 2)

    def mcopy(d):
        return rcopy(mix.at[fpeer(d)], rm.at[d], mix_s.at[d], mix_r.at[d], "frames", fpeer(d))

    def scopy(d):
        return rcopy(stat.at[fpeer(d)], rst.at[d], st_s.at[d], st_r.at[d], "frames", fpeer(d))

    def send_mix(d):
        scopy(d).start()
        mcopy(d).start()

    loop(1, nf, send_mix)
    rm[0] = mix[me]
    rst[0] = stat[me]
    loop(1, nf, lambda d: scopy(d).wait_recv())
    peak = rst[0, :, :128]
    for d in range(1, nf):
        peak = jnp.maximum(peak, rst[d, :, :128])
    loop(1, nf, lambda d: mcopy(d).wait_recv())
    num = [jnp.zeros((r, HDIM), F32) for _ in range(heads)]
    den = jnp.zeros((r, 128), F32)
    for d in range(nf):
        share = jnp.exp(rst[d, :, :128] - peak) * rst[d, :, 128:]
        den = den + share
        for h in range(heads):
            num[h] = num[h] + share[:, h:h + 1] * rm[d, :, h * HDIM:(h + 1) * HDIM].astype(F32)
    for h in range(heads):
        att_all[me, :, h * HDIM:(h + 1) * HDIM] = (num[h] / den[:, h:h + 1]).astype(BF16)

    def acopy(d):
        return rcopy(att_all.at[me], att_all.at[me], at_s.at[d], at_r.at[d], "frames", fpeer(d))

    loop(1, nf, lambda d: acopy(d).start())
    loop(1, nf, lambda d: acopy(d).wait_recv())

    copies[0].wait()
    att = flat(att_all[...])
    tile = tile_of(cols_d, 512)
    for t in range(cols_d // tile):
        cs = slice(t * tile, (t + 1) * tile)
        res = jnp.dot(att, wo[:, cs], preferred_element_type=F32)
        part[:, :, cs] = res.reshape(nh, latents // nh, tile).astype(BF16)

    def zcopy(d):
        return rcopy(part.at[zpeer(d)], rz.at[d], z_s.at[d], z_r.at[d], "heads", zpeer(d))

    loop(1, nh, lambda d: zcopy(d).start())
    loop(1, nh, lambda d: zcopy(d).wait_recv())
    state = part[hz].astype(F32)
    for d in range(1, nh):
        state = state + rz[d].astype(F32)
    lat_all[hz] = state.astype(BF16)

    def lcopy(d):
        return rcopy(lat_all.at[hz], lat_all.at[hz], l_s.at[d], l_r.at[d], "heads", zpeer(d))

    loop(1, nh, lambda d: lcopy(d).start())
    loop(1, nh, lambda d: lcopy(d).wait_recv())

    full = lat_all[...].astype(F32).reshape(latents, cols_d)
    nrm[...] = (full * gain[...]).astype(BF16)
    squares = jnp.sum(full * full, axis=1, keepdims=True)
    sqp[...] = jnp.broadcast_to(squares, (latents, 128)).reshape(nf, r, 128)

    def qcopy(d):
        return rcopy(sqp.at[fpeer(d)], rsq.at[d], sq_s.at[d], sq_r.at[d], "frames", fpeer(d))

    loop(1, nf, lambda d: qcopy(d).start())

    copies[1].wait()
    copies[2].wait()
    gt = tile_of(half, 512)

    def ccopy(t):
        return rcopy(gu.at[t, 1 - core], rc.at[t], c_s.at[t], c_r.at[t],
                     "frames", me + 1 - 2 * core)

    for t in range(2):
        for j in range(2):
            weight = (wg, wu)[j]

            def step(k, t=t, j=j, weight=weight):
                src = pl.ds(pl.multiple_of(t * half + k * gt, gt), gt)
                dst = pl.ds(pl.multiple_of(j * half + k * gt, gt), gt)
                res = jnp.dot(nrm[...], weight[:, src], preferred_element_type=F32)
                res = res.reshape(ny, nx, 2, r, gt).astype(BF16)
                for c in range(2):
                    gu[t, c, :, :, :, dst] = res[:, :, c]

            loop(0, half // gt, step)
        ccopy(t).start()

    def x2copy(d):
        return rcopy(gu.at[0, core, :, xpeer(d)], r2a.at[d], x2_s.at[d], x2_r.at[d],
                     "frames", xdev(xpeer(d)))

    def y2copy(d):
        return rcopy(gu.at[1, core, ypeer(d)], r2b.at[d], y2_s.at[d], y2_r.at[d],
                     "frames", ydev(ypeer(d)))

    def merge(t):
        ccopy(t).wait_recv()
        for y in range(ny):
            for x in range(nx):
                gu[t, core, y, x] = (
                    gu[t, core, y, x].astype(F32) + rc[t, y, x].astype(F32)).astype(BF16)

    merge(0)
    loop(1, nx, lambda d: x2copy(d).start())
    merge(1)
    loop(1, ny, lambda d: y2copy(d).start())

    def y3copy(d):
        return rcopy(s2a.at[ypeer(d)], r3a.at[d], y3_s.at[d], y3_r.at[d],
                     "frames", ydev(ypeer(d)))

    def x3copy(d):
        return rcopy(s2b.at[xpeer(d)], r3b.at[d], x3_s.at[d], x3_r.at[d],
                     "frames", xdev(xpeer(d)))

    loop(1, nx, lambda d: x2copy(d).wait_recv())
    for y in range(ny):
        total = gu[0, core, y, xi].astype(F32)
        for d in range(1, nx):
            total = total + r2a[d, y].astype(F32)
        s2a[y] = total.astype(BF16)
    loop(1, ny, lambda d: y3copy(d).start())
    loop(1, ny, lambda d: y2copy(d).wait_recv())
    for x in range(nx):
        total = gu[1, core, yi, x].astype(F32)
        for d in range(1, ny):
            total = total + r2b[d, x].astype(F32)
        s2b[x] = total.astype(BF16)
    loop(1, nx, lambda d: x3copy(d).start())

    loop(1, nf, lambda d: qcopy(d).wait_recv())
    ssum = sqp[me]
    for d in range(1, nf):
        ssum = ssum + rsq[d]
    scale = lax.rsqrt(ssum[:, :1] / (cols_d * nf) + norm_eps)

    def activate(t, total):
        gate = total[:, :half] * scale
        up = total[:, half:] * scale
        hid[t, core, yi, xi] = (gate / (1.0 + jnp.exp(-gate)) * up).astype(BF16)

    def hycopy(d):
        block = hid.at[0, core, yi, xi]
        return rcopy(block, block, hy_s.at[d], hy_r.at[d], "frames", ydev(ypeer(d)))

    def hxcopy(d):
        block = hid.at[1, core, yi, xi]
        return rcopy(block, block, hx_s.at[d], hx_r.at[d], "frames", xdev(xpeer(d)))

    def gxcopy(d):
        block = hid.at[0, core, :, xi]
        return rcopy(block, block, gx_s.at[d], gx_r.at[d], "frames", xdev(xpeer(d)))

    def gycopy(d):
        block = hid.at[1, core, yi]
        return rcopy(block, block, gy_s.at[d], gy_r.at[d], "frames", ydev(ypeer(d)))

    def hccopy(t):
        block = hid.at[t, core]
        return rcopy(block, block, hc_s.at[t], hc_r.at[t], "frames", me + 1 - 2 * core)

    loop(1, ny, lambda d: y3copy(d).wait_recv())
    total = s2a[yi].astype(F32)
    for d in range(1, ny):
        total = total + r3a[d].astype(F32)
    activate(0, total)
    loop(1, ny, lambda d: hycopy(d).start())
    loop(1, nx, lambda d: x3copy(d).wait_recv())
    total = s2b[xi].astype(F32)
    for d in range(1, nx):
        total = total + r3b[d].astype(F32)
    activate(1, total)
    loop(1, nx, lambda d: hxcopy(d).start())
    loop(1, ny, lambda d: hycopy(d).wait_recv())
    loop(1, nx, lambda d: gxcopy(d).start())
    loop(1, nx, lambda d: hxcopy(d).wait_recv())
    loop(1, ny, lambda d: gycopy(d).start())
    loop(1, nx, lambda d: gxcopy(d).wait_recv())
    hccopy(0).start()
    loop(1, ny, lambda d: gycopy(d).wait_recv())
    hccopy(1).start()
    copies[3].wait()
    hccopy(0).wait_recv()
    hccopy(1).wait_recv()

    dt = tile_of(cols_d, 256)

    def down(k):
        cs = pl.ds(pl.multiple_of(k * dt, dt), dt)
        res = jnp.dot(flat(hid[0]), wd[:half, cs], preferred_element_type=F32)
        res = res + jnp.dot(flat(hid[1]), wd[half:, cs], preferred_element_type=F32)
        res = res.reshape(2, nf // 2, r, dt).astype(BF16)
        for b in range(nf):
            dp[b, :, cs] = res[b % 2, b // 2]

    loop(0, cols_d // dt, down)

    def dcopy(d):
        return rcopy(dp.at[pl.ds(zpeer(d) * fh, fh)], rd.at[d], d_s.at[d], d_r.at[d],
                     "heads", zpeer(d))

    loop(1, nh, lambda d: dcopy(d).start())
    loop(1, nh, lambda d: dcopy(d).wait_recv())
    total = lat_all[hz].astype(F32).reshape(fh, r, cols_d) + dp[pl.ds(hz * fh, fh)].astype(F32)
    for d in range(1, nh):
        total = total + rd[d].astype(F32)
    out[...] = total.astype(BF16)

    def drain_f(d):
        scopy(d).wait_send()
        mcopy(d).wait_send()
        acopy(d).wait_send()
        qcopy(d).wait_send()

    def drain_z(d):
        zcopy(d).wait_send()
        lcopy(d).wait_send()
        dcopy(d).wait_send()

    def drain_x(d):
        x2copy(d).wait_send()
        x3copy(d).wait_send()
        hxcopy(d).wait_send()
        gxcopy(d).wait_send()

    def drain_y(d):
        y2copy(d).wait_send()
        y3copy(d).wait_send()
        hycopy(d).wait_send()
        gycopy(d).wait_send()

    loop(1, nf, drain_f)
    loop(1, nh, drain_z)
    loop(1, nx, drain_x)
    loop(1, ny, drain_y)
    for t in range(2):
        ccopy(t).wait_send()
        hccopy(t).wait_send()


def solution(mesh):
    nf, nh = mesh.shape["frames"], mesh.shape["heads"]
    chips = nf // 2
    nx = max(k for k in range(1, math.isqrt(chips) + 1) if chips % k == 0)
    ny = chips // nx
    vmem = pl.BlockSpec(memory_space=pltpu.VMEM)
    any_ = pl.BlockSpec(memory_space=pl.ANY)
    dma = pltpu.SemaphoreType.DMA

    def on_device(frames, latents, w_query, w_key, w_value, w_out, norm_gain, w_gate, w_up, w_down):
        tokens, feats = frames.shape
        r = latents.shape[0]
        width = w_key.shape[1]
        rows = r * nf
        mix, stat = pl.pallas_call(
            lambda *refs: attend_kernel(nf, nh, *refs),
            out_shape=[
                jax.ShapeDtypeStruct((rows, width), BF16),
                jax.ShapeDtypeStruct((rows, 256), F32),
            ],
            in_specs=[vmem, vmem, any_, any_, any_],
            out_specs=[vmem, vmem],
            scratch_shapes=[
                pltpu.VMEM((nh, tokens, feats), BF16),
                pltpu.VMEM((nf, r, width), BF16),
                pltpu.VMEM(w_query.shape, BF16),
                pltpu.VMEM((2, nh, feats, width), BF16),
                pltpu.VMEM((2, tokens, width), F32),
                dma((3,)), dma((nh,)), dma((nh,)), dma((nh,)), dma((nf,)), dma((nf,)),
            ],
            compiler_params=pltpu.CompilerParams(
                collective_id=0, has_side_effects=True, vmem_limit_bytes=48 * MIB),
            name="attend",
        )(
            frames, latents, w_query,
            w_key.reshape(nh, feats, width), w_value.reshape(nh, feats, width),
        )
        cols_d = w_out.shape[1]
        units = w_gate.shape[1]
        half = units // 2
        fh = nf // nh
        out = pl.pallas_call(
            lambda *refs: block_kernel(nf, nh, ny, nx, *refs),
            out_shape=jax.ShapeDtypeStruct((fh, r, cols_d), BF16),
            in_specs=[vmem, vmem, vmem, any_, any_, any_, any_],
            out_specs=vmem,
            scratch_shapes=[
                pltpu.VMEM(w_out.shape, BF16),
                pltpu.VMEM(w_gate.shape, BF16),
                pltpu.VMEM(w_up.shape, BF16),
                pltpu.VMEM(w_down.shape, BF16),
                pltpu.VMEM((nf, r, width), BF16),
                pltpu.VMEM((nf, r, 256), F32),
                pltpu.VMEM((nf, r, width), BF16),
                pltpu.VMEM((nh, rows // nh, cols_d), BF16),
                pltpu.VMEM((nh, rows // nh, cols_d), BF16),
                pltpu.VMEM((nh, rows // nh, cols_d), BF16),
                pltpu.VMEM((rows, cols_d), BF16),
                pltpu.VMEM((nf, r, 128), F32),
                pltpu.VMEM((nf, r, 128), F32),
                pltpu.VMEM((2, 2, ny, nx, r, units), BF16),
                pltpu.VMEM((2, ny, nx, r, units), BF16),
                pltpu.VMEM((nx, ny, r, units), BF16),
                pltpu.VMEM((ny, nx, r, units), BF16),
                pltpu.VMEM((ny, r, units), BF16),
                pltpu.VMEM((nx, r, units), BF16),
                pltpu.VMEM((ny, r, units), BF16),
                pltpu.VMEM((nx, r, units), BF16),
                pltpu.VMEM((2, 2, ny, nx, r, half), BF16),
                pltpu.VMEM((nf, r, cols_d), BF16),
                pltpu.VMEM((nh, fh, r, cols_d), BF16),
                dma((4,)),
                *[dma((n,)) for n in (
                    nf, nf, nf, nf, nf, nf, nh, nh, nh, nh, nf, nf,
                    2, 2, nx, nx, ny, ny, nx, nx, ny, ny,
                    ny, ny, nx, nx, nx, nx, ny, ny, 2, 2, nh, nh)],
            ],
            compiler_params=pltpu.CompilerParams(
                collective_id=1, has_side_effects=True, vmem_limit_bytes=58 * MIB),
            name="block",
        )(
            mix.reshape(nf, r, width), stat.reshape(nf, r, 256),
            norm_gain.reshape(1, -1), w_out, w_gate, w_up, w_down,
        )
        return out.reshape(rows // nh, cols_d)

    placed = (
        P("frames", "heads"), P("frames", None), P(None, "heads"), P(None, "heads"),
        P(None, "heads"), P("heads", "frames"), P("frames"), P("frames", "heads"),
        P("frames", "heads"), P("heads", "frames"),
    )
    return jax.shard_map(
        on_device, mesh=mesh, in_specs=placed, out_specs=P("heads", "frames"), check_vma=False
    )
```

time: 382 us -> 179 us (0.47)
  waiting for transfers between devices: 243 us -> 0 us
  Pallas kernels: 0 us -> 169 us
  blocking collectives: 63.6 us -> 0 us
  matrix products: 45.6 us -> 0 us
  between operations: 13.6 us -> 0.04 us
  other arithmetic: 11.1 us -> 0 us
  local copies, waits for them, and re-layouts: 0.02 us -> 7.01 us
    pallas_call x0 -> x2, Pallas kernels: none -> 169 us  [the longest x1 105 us: on_device(): pl.pallas_call(lambda *refs: block_kernel(nf, nh, ny, nx, *refs), out_sha...]
    reduce_scatter x4 -> x0, waiting for transfers between devices: 137 us -> none  [the longest x1 54.6 us: on_device(): lax.psum_scatter(gate_part, 'frames', scatter_dimension=0, tiled=True)]
    all_gather x2 -> x0, waiting for transfers between devices: 66.6 us -> none  [the longest x1 38.6 us: on_device(): piece = lax.all_gather(frames, 'heads', axis=1, tiled=True)]
    dot_general x9 -> x0, matrix products: 45.6 us -> none  [the longest x1 7.69 us: on_device(): gate_part = jnp.dot(normed, w_gate, preferred_element_type=jnp.float32)]
    psum x1 -> x0, waiting for transfers between devices: 38.9 us -> none  [on_device(): total_all, mixed_all = lax.psum((total, mixed), 'frames')]
    all_gather x2 -> x0, blocking collectives: 25.4 us -> none  [the longest x1 15.5 us: on_device(): latent_full = lax.all_gather(latent_state, 'heads', axis=0, tiled=True)]
    psum x2 -> x0, blocking collectives: 24 us -> none  [the longest x1 12.2 us: on_device(): total_all, mixed_all = lax.psum((total, mixed), 'frames')]
    pmax x1 -> x0, blocking collectives: 14.3 us -> none  [on_device(): score_peak = lax.pmax(local_max, 'frames')]
  transfers between devices with their start and end apart: 7 -> 0, of which waited for: 7 -> 0; matrix products, arithmetic and copies ran while one was open for 4% -> 0% of each run, Pallas kernels for 0% -> 0%
where the time goes in v1:
time: 179 us; the launch traced here: 176 us
  Pallas kernels  169 us (94%)
  local copies, waits for them, and re-layouts  7.01 us (4%)
    pallas_call x1, Pallas kernels, on_device(): pl.pallas_call(lambda *refs: block_kernel(nf, nh, ny, nx, *refs), out_sha...  105 us
    pallas_call x1, Pallas kernels, on_device(): pl.pallas_call(lambda *refs: attend_kernel(nf, nh, *refs), out_shape=[jax...  63.4 us
    unnamed x10, local copies, waits for them, and re-layouts  7.01 us

profile of v1, /device:TPU:24, one launch (start us, length us, event | category | flops | bytes accessed | tf_op | source)
XLA Modules:
  0.0 175.9 jit_solution(9966037424052099897)
XLA Ops:
  0.0 1.4 copy.11.refs_0_
  1.4 0.0 copy-start
  1.4 1.7 copy-done
  3.1 0.0 copy-start.3
  3.1 0.9 copy-done.3
  4.0 63.4 %attend.1 = (bf16[256,1024]{1,0:T(8,128)(2,1)S(1)}, f32[256,256]{1,0:T(8,128)S(1)}) custom-call(bf16[1024,288]{1,0:T(8,128)(2,1)S(1)} %copy.11.refs_0_, bf16[32,1152]{1,0:T(8,128)(2,1)S(1)} %copy-done.3, bf16[1152,1024]{1,0:T(8,128)(2,1)S(1)} %copy-done, bf16[4,288,1024]{2,1,0:T(8,128)(2,1)} %bitcast.8, bf16[4,288,1024]{2,1,0:T(8,128)(2,1)} %bitcast.9), custom_call_target="tpu_custom_call" | custom-call | tf_op jit(solution)/shard_map/attend/pallas_call | solution.py:519
  67.4 0.0 copy-start.1
  67.4 0.8 copy-done.1
  68.2 0.0 copy-start.2
  68.2 0.7 copy-done.2
  68.9 105.4 %block.1 = bf16[2,32,1024]{2,1,0:T(8,128)(2,1)} custom-call(bf16[8,32,1024]{2,1,0:T(8,128)(2,1)} %bitcast.6, f32[8,32,256]{2,1,0:T(8,128)} %bitcast.7, f32[1,1024]{1,0:T(1,128)} %bitcast.11, bf16[1024,1024]{1,0:T(8,128)(2,1)} %refs_3_.1, bf16[1024,4096]{1,0:T(8,128)(2,1)} %refs_4_.1, bf16[1024,4096]{1,0:T(8,128)(2,1)} %refs_5_.1, bf16[4096,1024]{1,0:T(8,128)(2,1)} %refs_6_.1), custom_call_target="tpu_custom_call" | custom-call | tf_op jit(solution)/shard_map/block/pallas_call | solution.py:546
  174.3 1.6 copy.13
Async XLA Ops:
  1.4 1.7 copy-start
  3.1 0.9 copy-start.3
  67.4 0.8 copy-start.1
  68.2 0.7 copy-start.2

commit v2 on v1

v2 whole, which is shorter than its diff:
```python
import math

import jax
import jax.numpy as jnp
from jax import lax
from jax.experimental import pallas as pl
from jax.experimental.pallas import tpu as pltpu
from jax.sharding import PartitionSpec as P

HDIM = 128
norm_eps = 1e-06
F32 = jnp.float32
BF16 = jnp.bfloat16
MIB = 2**20


def rcopy(src, dst, ssem, rsem, axis, peer):
    return pltpu.make_async_remote_copy(
        src_ref=src,
        dst_ref=dst,
        send_sem=ssem,
        recv_sem=rsem,
        device_id={axis: peer},
        device_id_type=pl.DeviceIdType.MESH,
    )


def loop(lo, hi, body):
    def step(i, carry):
        body(i)
        return carry

    lax.fori_loop(lo, hi, step, 0)


def flat(value):
    rows, cols = value.shape[-2], value.shape[-1]
    if rows % 16:
        return value.astype(F32).reshape(-1, cols).astype(value.dtype)
    return value.reshape(-1, cols)


def tile_of(size, want):
    return want if size % want == 0 else size


def attend_kernel(
    nf, nh, ng,
    fr, lat, wq, wk, wv,
    mix_out, stat_out,
    fr_all, q_all, wq_v, wkv, acc,
    w_sem, rs_sem, ls_sem, fr_sem, qs_sem, qr_sem,
):
    me = lax.axis_index("frames")
    hz = lax.axis_index("heads")
    width = wq.shape[1]
    heads = width // HDIM
    tokens = fr.shape[0]

    c_q = pltpu.make_async_copy(wq, wq_v, w_sem.at[0])
    c_k = pltpu.make_async_copy(wk, wkv.at[0], w_sem.at[1])
    c_v = pltpu.make_async_copy(wv, wkv.at[1], w_sem.at[2])
    c_q.start()
    c_k.start()
    c_v.start()

    barrier = pltpu.get_barrier_semaphore()

    def greet(d):
        pl.semaphore_signal(
            barrier, inc=1, device_id={"frames": lax.rem(me + d, nf)},
            device_id_type=pl.DeviceIdType.MESH)

    loop(1, nf, greet)
    has_l = hz > 0
    has_r = hz < nh - 1

    @pl.when(has_l)
    def _():
        pl.semaphore_signal(barrier, inc=1, device_id={"heads": hz - 1},
                            device_id_type=pl.DeviceIdType.MESH)

    @pl.when(has_r)
    def _():
        pl.semaphore_signal(barrier, inc=1, device_id={"heads": hz + 1},
                            device_id_type=pl.DeviceIdType.MESH)

    pl.semaphore_wait(barrier, nf - 1 + has_l.astype(jnp.int32) + has_r.astype(jnp.int32))

    def right(s, src, b):
        return rcopy(src, fr_all.at[b], rs_sem.at[s], fr_sem.at[b], "heads", hz + 1)

    def left(s, src, b):
        return rcopy(src, fr_all.at[b], ls_sem.at[s], fr_sem.at[b], "heads", hz - 1)

    @pl.when(has_r)
    def _():
        right(0, fr, hz).start()

    @pl.when(has_l)
    def _():
        left(0, fr, hz).start()

    c_q.wait()
    fh = nf // nh
    per = fh // ng
    inner = lax.rem(me, fh)
    slot = (inner // per * nh + me // fh) * per + lax.rem(inner, per)
    q_all[slot] = jnp.dot(lat[...], wq_v[...], preferred_element_type=F32).astype(BF16)

    def qcopy(d):
        return rcopy(q_all.at[slot], q_all.at[slot], qs_sem.at[d], qr_sem.at[d],
                     "frames", lax.rem(me + d, nf))

    loop(1, nf, lambda d: qcopy(d).start())
    c_k.wait()
    c_v.wait()

    tt = tile_of(tokens, 256)

    def project(x, b, first):
        def tile(i):
            rows = pl.ds(pl.multiple_of(i * tt, tt), tt)
            xb = x[rows, :]
            for w in range(2):
                term = jnp.dot(xb, wkv[w, b], preferred_element_type=F32)
                if first:
                    acc[w, rows, :] = term
                else:
                    acc[w, rows, :] += term
        loop(0, tokens // tt, tile)

    project(fr, hz, True)

    def hop(s):
        lb, rb = hz - s, hz + s

        @pl.when(lb >= 0)
        def _():
            right(s, fr, lb).wait_recv()

            @pl.when(has_r)
            def _():
                right(s, fr_all.at[lb], lb).start()

        @pl.when(rb < nh)
        def _():
            right(s, fr, rb).wait_recv()

            @pl.when(has_l)
            def _():
                left(s, fr_all.at[rb], rb).start()

        @pl.when(lb >= 0)
        def _():
            project(fr_all.at[lb], lb, False)

        @pl.when(rb < nh)
        def _():
            project(fr_all.at[rb], rb, False)

    loop(1, nh, hop)
    loop(1, nf, lambda d: qcopy(d).wait_recv())

    scale = HDIM ** (-0.5)
    latents = mix_out.shape[0]
    lane = lax.broadcasted_iota(jnp.int32, (latents, 128), 1)
    peaks = jnp.zeros((latents, 128), F32)
    sums = jnp.ones((latents, 128), F32)
    for h in range(heads):
        cols = slice(h * HDIM, (h + 1) * HDIM)
        q = flat(q_all[:, :, cols])
        k = acc[0, :, cols].astype(BF16)
        v = acc[1, :, cols].astype(BF16)
        scores = lax.dot_general(q, k, (((1,), (1,)), ((), ())),
                                 preferred_element_type=F32) * scale
        peak = jnp.max(scores, axis=1, keepdims=True)
        weights = jnp.exp(scores - peak)
        total = jnp.sum(weights, axis=1, keepdims=True)
        mixed = jnp.dot(weights.astype(BF16), v, preferred_element_type=F32)
        mix_out[:, cols] = (mixed / total).astype(BF16)
        peaks = jnp.where(lane == h, peak, peaks)
        sums = jnp.where(lane == h, total, sums)
    stat_out[:, :128] = peaks
    stat_out[:, 128:] = sums

    loop(1, nf, lambda d: qcopy(d).wait_send())

    def drain(s):
        @pl.when((hz - s >= 0) & has_r)
        def _():
            right(s, fr, hz).wait_send()

        @pl.when((hz + s < nh) & has_l)
        def _():
            left(s, fr, hz).wait_send()

    loop(0, nh, drain)


def block_kernel(
    nf, nh, ng, ny, nx,
    mix, stat, gain, w_out, w_gate, w_up, w_down,
    out,
    wo, wg, wu, wd,
    rm, rst, att_all, part, rz, lat_all, nrm, sqp, rsq,
    gu, rc, r2a, r2b, s2a, s2b, r3a, r3b, hid, dp, rd,
    w_sem, mix_s, mix_r, st_s, st_r, at_s, at_r, z_s, z_r, l_s, l_r, sq_s, sq_r,
    c_s, c_r, x2_s, x2_r, y2_s, y2_r, x3_s, x3_r, y3_s, y3_r,
    hy_s, hy_r, hx_s, hx_r, gx_s, gx_r, gy_s, gy_r, hc_s, hc_r, d_s, d_r,
):
    me = lax.axis_index("frames")
    hz = lax.axis_index("heads")
    core = lax.rem(me, 2)
    xi = lax.rem(me // 2, nx)
    yi = me // (2 * nx)
    r, width = mix.shape[2], mix.shape[3]
    heads = width // HDIM
    fh = nf // nh
    cols_d = wo.shape[1]
    units = wg.shape[1]
    half = units // 2
    latents = nf * r

    copies = [
        pltpu.make_async_copy(src, dst, w_sem.at[i])
        for i, (src, dst) in enumerate(
            [(w_out, wo), (w_gate, wg), (w_up, wu), (w_down, wd)])
    ]
    for c in copies:
        c.start()

    barrier = pltpu.get_barrier_semaphore()

    def fpeer(d):
        return lax.rem(me + d, nf)

    def zpeer(d):
        return lax.rem(hz + d, nh)

    def xpeer(d):
        return lax.rem(xi + d, nx)

    def ypeer(d):
        return lax.rem(yi + d, ny)

    def xdev(x):
        return (yi * nx + x) * 2 + core

    def ydev(y):
        return (y * nx + xi) * 2 + core

    def greet_f(d):
        pl.semaphore_signal(barrier, inc=1, device_id={"frames": fpeer(d)},
                            device_id_type=pl.DeviceIdType.MESH)

    def greet_z(d):
        pl.semaphore_signal(barrier, inc=1, device_id={"heads": zpeer(d)},
                            device_id_type=pl.DeviceIdType.MESH)

    loop(1, nf, greet_f)
    loop(1, nh, greet_z)
    pl.semaphore_wait(barrier, nf + nh - 2)

    def phases(
        g,
        mix, stat, out, rm, rst, att_all, part, rz, lat_all, nrm, sqp, rsq, gu, rc, r2a, r2b,
        s2a, s2b, r3a, r3b, hid, dp, rd, mix_s, mix_r, st_s, st_r, at_s, at_r, z_s, z_r, l_s,
        l_r, sq_s, sq_r, c_s, c_r, x2_s, x2_r, y2_s, y2_r, x3_s, x3_r, y3_s, y3_r, hy_s, hy_r,
        hx_s, hx_r, gx_s, gx_r, gy_s, gy_r, hc_s, hc_r, d_s, d_r,
    ):
        def mcopy(d):
            return rcopy(mix.at[fpeer(d)], rm.at[d], mix_s.at[d], mix_r.at[d], "frames", fpeer(d))

        def scopy(d):
            return rcopy(stat.at[fpeer(d)], rst.at[d], st_s.at[d], st_r.at[d], "frames", fpeer(d))

        def send_mix(d):
            scopy(d).start()
            mcopy(d).start()

        loop(1, nf, send_mix)
        rm[0] = mix[me]
        rst[0] = stat[me]
        yield
        loop(1, nf, lambda d: scopy(d).wait_recv())
        peak = rst[0, :, :128]
        for d in range(1, nf):
            peak = jnp.maximum(peak, rst[d, :, :128])
        loop(1, nf, lambda d: mcopy(d).wait_recv())
        num = [jnp.zeros((r, HDIM), F32) for _ in range(heads)]
        den = jnp.zeros((r, 128), F32)
        for d in range(nf):
            share = jnp.exp(rst[d, :, :128] - peak) * rst[d, :, 128:]
            den = den + share
            for h in range(heads):
                num[h] = num[h] + share[:, h:h + 1] * rm[d, :, h * HDIM:(h + 1) * HDIM].astype(F32)
        for h in range(heads):
            att_all[me, :, h * HDIM:(h + 1) * HDIM] = (num[h] / den[:, h:h + 1]).astype(BF16)

        def acopy(d):
            return rcopy(att_all.at[me], att_all.at[me], at_s.at[d], at_r.at[d], "frames", fpeer(d))

        loop(1, nf, lambda d: acopy(d).start())
        yield
        loop(1, nf, lambda d: acopy(d).wait_recv())

        if g == 0:
            copies[0].wait()
        att = flat(att_all[...])
        tile = tile_of(cols_d, 512)
        for t in range(cols_d // tile):
            cs = slice(t * tile, (t + 1) * tile)
            res = jnp.dot(att, wo[:, cs], preferred_element_type=F32)
            part[:, :, cs] = res.reshape(nh, latents // nh, tile).astype(BF16)

        def zcopy(d):
            return rcopy(part.at[zpeer(d)], rz.at[d], z_s.at[d], z_r.at[d], "heads", zpeer(d))

        loop(1, nh, lambda d: zcopy(d).start())
        yield
        loop(1, nh, lambda d: zcopy(d).wait_recv())
        state = part[hz].astype(F32)
        for d in range(1, nh):
            state = state + rz[d].astype(F32)
        lat_all[hz] = state.astype(BF16)

        def lcopy(d):
            return rcopy(lat_all.at[hz], lat_all.at[hz], l_s.at[d], l_r.at[d], "heads", zpeer(d))

        loop(1, nh, lambda d: lcopy(d).start())
        yield
        loop(1, nh, lambda d: lcopy(d).wait_recv())

        full = lat_all[...].astype(F32).reshape(latents, cols_d)
        nrm[...] = (full * gain[...]).astype(BF16)
        squares = jnp.sum(full * full, axis=1, keepdims=True)
        sqp[...] = jnp.broadcast_to(squares, (latents, 128)).reshape(nf, r, 128)

        def qcopy(d):
            return rcopy(sqp.at[fpeer(d)], rsq.at[d], sq_s.at[d], sq_r.at[d], "frames", fpeer(d))

        loop(1, nf, lambda d: qcopy(d).start())

        if g == 0:
            copies[1].wait()
            copies[2].wait()
        gt = tile_of(half, 512)

        def ccopy(t):
            return rcopy(gu.at[t, 1 - core], rc.at[t], c_s.at[t], c_r.at[t],
                         "frames", me + 1 - 2 * core)

        for t in range(2):
            for j in range(2):
                weight = (wg, wu)[j]

                def step(k, t=t, j=j, weight=weight):
                    src = pl.ds(pl.multiple_of(t * half + k * gt, gt), gt)
                    dst = pl.ds(pl.multiple_of(j * half + k * gt, gt), gt)
                    res = jnp.dot(nrm[...], weight[:, src], preferred_element_type=F32)
                    res = res.reshape(ny, nx, 2, r, gt).astype(BF16)
                    for c in range(2):
                        gu[t, c, :, :, :, dst] = res[:, :, c]

                loop(0, half // gt, step)
            ccopy(t).start()
        yield

        def x2copy(d):
            return rcopy(gu.at[0, core, :, xpeer(d)], r2a.at[d], x2_s.at[d], x2_r.at[d],
                         "frames", xdev(xpeer(d)))

        def y2copy(d):
            return rcopy(gu.at[1, core, ypeer(d)], r2b.at[d], y2_s.at[d], y2_r.at[d],
                         "frames", ydev(ypeer(d)))

        def merge(t):
            ccopy(t).wait_recv()
            for y in range(ny):
                for x in range(nx):
                    gu[t, core, y, x] = (
                        gu[t, core, y, x].astype(F32) + rc[t, y, x].astype(F32)).astype(BF16)

        merge(0)
        loop(1, nx, lambda d: x2copy(d).start())
        merge(1)
        loop(1, ny, lambda d: y2copy(d).start())
        yield

        def y3copy(d):
            return rcopy(s2a.at[ypeer(d)], r3a.at[d], y3_s.at[d], y3_r.at[d],
                         "frames", ydev(ypeer(d)))

        def x3copy(d):
            return rcopy(s2b.at[xpeer(d)], r3b.at[d], x3_s.at[d], x3_r.at[d],
                         "frames", xdev(xpeer(d)))

        loop(1, nx, lambda d: x2copy(d).wait_recv())
        for y in range(ny):
            total = gu[0, core, y, xi].astype(F32)
            for d in range(1, nx):
                total = total + r2a[d, y].astype(F32)
            s2a[y] = total.astype(BF16)
        loop(1, ny, lambda d: y3copy(d).start())
        loop(1, ny, lambda d: y2copy(d).wait_recv())
        for x in range(nx):
            total = gu[1, core, yi, x].astype(F32)
            for d in range(1, ny):
                total = total + r2b[d, x].astype(F32)
            s2b[x] = total.astype(BF16)
        loop(1, nx, lambda d: x3copy(d).start())
        yield

        loop(1, nf, lambda d: qcopy(d).wait_recv())
        ssum = sqp[me]
        for d in range(1, nf):
            ssum = ssum + rsq[d]
        scale = lax.rsqrt(ssum[:, :1] / (cols_d * nf) + norm_eps)

        def activate(t, total):
            gate = total[:, :half] * scale
            up = total[:, half:] * scale
            hid[t, core, yi, xi] = (gate / (1.0 + jnp.exp(-gate)) * up).astype(BF16)

        def hycopy(d):
            block = hid.at[0, core, yi, xi]
            return rcopy(block, block, hy_s.at[d], hy_r.at[d], "frames", ydev(ypeer(d)))

        def hxcopy(d):
            block = hid.at[1, core, yi, xi]
            return rcopy(block, block, hx_s.at[d], hx_r.at[d], "frames", xdev(xpeer(d)))

        def gxcopy(d):
            block = hid.at[0, core, :, xi]
            return rcopy(block, block, gx_s.at[d], gx_r.at[d], "frames", xdev(xpeer(d)))

        def gycopy(d):
            block = hid.at[1, core, yi]
            return rcopy(block, block, gy_s.at[d], gy_r.at[d], "frames", ydev(ypeer(d)))

        def hccopy(t):
            block = hid.at[t, core]
            return rcopy(block, block, hc_s.at[t], hc_r.at[t], "frames", me + 1 - 2 * core)

        loop(1, ny, lambda d: y3copy(d).wait_recv())
        total = s2a[yi].astype(F32)
        for d in range(1, ny):
            total = total + r3a[d].astype(F32)
        activate(0, total)
        loop(1, ny, lambda d: hycopy(d).start())
        loop(1, nx, lambda d: x3copy(d).wait_recv())
        total = s2b[xi].astype(F32)
        for d in range(1, nx):
            total = total + r3b[d].astype(F32)
        activate(1, total)
        loop(1, nx, lambda d: hxcopy(d).start())
        yield
        loop(1, ny, lambda d: hycopy(d).wait_recv())
        loop(1, nx, lambda d: gxcopy(d).start())
        loop(1, nx, lambda d: hxcopy(d).wait_recv())
        loop(1, ny, lambda d: gycopy(d).start())
        yield
        loop(1, nx, lambda d: gxcopy(d).wait_recv())
        hccopy(0).start()
        loop(1, ny, lambda d: gycopy(d).wait_recv())
        hccopy(1).start()
        yield
        if g == 0:
            copies[3].wait()
        hccopy(0).wait_recv()
        hccopy(1).wait_recv()

        dt = tile_of(cols_d, 256)

        def down(k):
            cs = pl.ds(pl.multiple_of(k * dt, dt), dt)
            res = jnp.dot(flat(hid[0]), wd[:half, cs], preferred_element_type=F32)
            res = res + jnp.dot(flat(hid[1]), wd[half:, cs], preferred_element_type=F32)
            res = res.reshape(2, nf // 2, r, dt).astype(BF16)
            for b in range(nf):
                dp[b, :, cs] = res[b % 2, b // 2]

        loop(0, cols_d // dt, down)

        def dcopy(d):
            return rcopy(dp.at[pl.ds(zpeer(d) * fh, fh)], rd.at[d], d_s.at[d], d_r.at[d],
                         "heads", zpeer(d))

        loop(1, nh, lambda d: dcopy(d).start())
        yield
        loop(1, nh, lambda d: dcopy(d).wait_recv())
        total = lat_all[hz].astype(F32).reshape(fh, r, cols_d) + dp[pl.ds(hz * fh, fh)].astype(F32)
        for d in range(1, nh):
            total = total + rd[d].astype(F32)
        out[...] = total.astype(BF16)

        def drain_f(d):
            scopy(d).wait_send()
            mcopy(d).wait_send()
            acopy(d).wait_send()
            qcopy(d).wait_send()

        def drain_z(d):
            zcopy(d).wait_send()
            lcopy(d).wait_send()
            dcopy(d).wait_send()

        def drain_x(d):
            x2copy(d).wait_send()
            x3copy(d).wait_send()
            hxcopy(d).wait_send()
            gxcopy(d).wait_send()

        def drain_y(d):
            y2copy(d).wait_send()
            y3copy(d).wait_send()
            hycopy(d).wait_send()
            gycopy(d).wait_send()

        loop(1, nf, drain_f)
        loop(1, nh, drain_z)
        loop(1, nx, drain_x)
        loop(1, ny, drain_y)
        for t in range(2):
            ccopy(t).wait_send()
            hccopy(t).wait_send()

    views = [
        mix, stat, out, rm, rst, att_all, part, rz, lat_all, nrm, sqp, rsq, gu, rc, r2a, r2b,
        s2a, s2b, r3a, r3b, hid, dp, rd, mix_s, mix_r, st_s, st_r, at_s, at_r, z_s, z_r, l_s,
        l_r, sq_s, sq_r, c_s, c_r, x2_s, x2_r, y2_s, y2_r, x3_s, x3_r, y3_s, y3_r, hy_s, hy_r,
        hx_s, hx_r, gx_s, gx_r, gy_s, gy_r, hc_s, hc_r, d_s, d_r,
    ]
    running = [phases(g, *[v.at[g] for v in views]) for g in range(ng)]
    while running:
        running = [p for p in running if next(p, running) is None]


def solution(mesh):
    nf, nh = mesh.shape["frames"], mesh.shape["heads"]
    chips = nf // 2
    nx = max(k for k in range(1, math.isqrt(chips) + 1) if chips % k == 0)
    ny = chips // nx
    vmem = pl.BlockSpec(memory_space=pltpu.VMEM)
    any_ = pl.BlockSpec(memory_space=pl.ANY)
    dma = pltpu.SemaphoreType.DMA

    def on_device(frames, latents, w_query, w_key, w_value, w_out, norm_gain, w_gate, w_up, w_down):
        tokens, feats = frames.shape
        r = latents.shape[0]
        width = w_key.shape[1]
        rows = r * nf
        ng = 2 if (nf // nh) % 2 == 0 and r % 32 == 0 else 1
        rg = r // ng
        mix, stat = pl.pallas_call(
            lambda *refs: attend_kernel(nf, nh, ng, *refs),
            out_shape=[
                jax.ShapeDtypeStruct((rows, width), BF16),
                jax.ShapeDtypeStruct((rows, 256), F32),
            ],
            in_specs=[vmem, vmem, any_, any_, any_],
            out_specs=[vmem, vmem],
            scratch_shapes=[
                pltpu.VMEM((nh, tokens, feats), BF16),
                pltpu.VMEM((nf, r, width), BF16),
                pltpu.VMEM(w_query.shape, BF16),
                pltpu.VMEM((2, nh, feats, width), BF16),
                pltpu.VMEM((2, tokens, width), F32),
                dma((3,)), dma((nh,)), dma((nh,)), dma((nh,)), dma((nf,)), dma((nf,)),
            ],
            compiler_params=pltpu.CompilerParams(
                collective_id=0, has_side_effects=True, vmem_limit_bytes=48 * MIB),
            name="attend",
        )(
            frames, latents, w_query,
            w_key.reshape(nh, feats, width), w_value.reshape(nh, feats, width),
        )
        cols_d = w_out.shape[1]
        units = w_gate.shape[1]
        half = units // 2
        fh = nf // nh
        out = pl.pallas_call(
            lambda *refs: block_kernel(nf, nh, ng, ny, nx, *refs),
            out_shape=jax.ShapeDtypeStruct((ng, fh, rg, cols_d), BF16),
            in_specs=[vmem, vmem, vmem, any_, any_, any_, any_],
            out_specs=vmem,
            scratch_shapes=[
                pltpu.VMEM(w_out.shape, BF16),
                pltpu.VMEM(w_gate.shape, BF16),
                pltpu.VMEM(w_up.shape, BF16),
                pltpu.VMEM(w_down.shape, BF16),
                pltpu.VMEM((ng, nf, rg, width), BF16),
                pltpu.VMEM((ng, nf, rg, 256), F32),
                pltpu.VMEM((ng, nf, rg, width), BF16),
                pltpu.VMEM((ng, nh, rows // ng // nh, cols_d), BF16),
                pltpu.VMEM((ng, nh, rows // ng // nh, cols_d), BF16),
                pltpu.VMEM((ng, nh, rows // ng // nh, cols_d), BF16),
                pltpu.VMEM((ng, rows // ng, cols_d), BF16),
                pltpu.VMEM((ng, nf, rg, 128), F32),
                pltpu.VMEM((ng, nf, rg, 128), F32),
                pltpu.VMEM((ng, 2, 2, ny, nx, rg, units), BF16),
                pltpu.VMEM((ng, 2, ny, nx, rg, units), BF16),
                pltpu.VMEM((ng, nx, ny, rg, units), BF16),
                pltpu.VMEM((ng, ny, nx, rg, units), BF16),
                pltpu.VMEM((ng, ny, rg, units), BF16),
                pltpu.VMEM((ng, nx, rg, units), BF16),
                pltpu.VMEM((ng, ny, rg, units), BF16),
                pltpu.VMEM((ng, nx, rg, units), BF16),
                pltpu.VMEM((ng, 2, 2, ny, nx, rg, half), BF16),
                pltpu.VMEM((ng, nf, rg, cols_d), BF16),
                pltpu.VMEM((ng, nh, fh, rg, cols_d), BF16),
                dma((4,)),
                *[dma((ng, n)) for n in (
                    nf, nf, nf, nf, nf, nf, nh, nh, nh, nh, nf, nf,
                    2, 2, nx, nx, ny, ny, nx, nx, ny, ny,
                    ny, ny, nx, nx, nx, nx, ny, ny, 2, 2, nh, nh)],
            ],
            compiler_params=pltpu.CompilerParams(
                collective_id=1, has_side_effects=True, vmem_limit_bytes=58 * MIB),
            name="block",
        )(
            mix.reshape(ng, nf, rg, width), stat.reshape(ng, nf, rg, 256),
            norm_gain.reshape(1, -1), w_out, w_gate, w_up, w_down,
        )
        return out.reshape(rows // nh, cols_d)

    placed = (
        P("frames", "heads"), P("frames", None), P(None, "heads"), P(None, "heads"),
        P(None, "heads"), P("heads", "frames"), P("frames"), P("frames", "heads"),
        P("frames", "heads"), P("heads", "frames"),
    )
    return jax.shard_map(
        on_device, mesh=mesh, in_specs=placed, out_specs=P("heads", "frames"), check_vma=False
    )
```

time: 179 us -> 166 us (0.927); the launches traced: 176 us -> 166 us
  Pallas kernels: 169 us -> 159 us
    pallas_call x2, Pallas kernels: 169 us -> 159 us  [the longest x1 95.6 us: on_device(): pl.pallas_call(lambda *refs: block_kernel(nf, nh, ng, ny, nx, *refs), out...]
where the time goes in v2:
time: 166 us
  Pallas kernels  159 us (96%)
  local copies, waits for them, and re-layouts  7.01 us (4%)
    pallas_call x1, Pallas kernels, on_device(): pl.pallas_call(lambda *refs: block_kernel(nf, nh, ng, ny, nx, *refs), out...  95.6 us
    pallas_call x1, Pallas kernels, on_device(): pl.pallas_call(lambda *refs: attend_kernel(nf, nh, ng, *refs), out_shape=...  63.4 us
    unnamed x10, local copies, waits for them, and re-layouts  7.01 us

profile of v2, /device:TPU:24, one launch (start us, length us, event | category | flops | bytes accessed | tf_op | source)
XLA Modules:
  0.0 166.1 jit_solution(1958605789772813423)
XLA Ops:
  0.0 1.4 copy.11.refs_0_
  1.4 0.0 copy-start
  1.4 1.7 copy-done
  3.1 0.0 copy-start.3
  3.1 0.9 copy-done.3
  4.0 63.4 %attend.1 = (bf16[256,1024]{1,0:T(8,128)(2,1)S(1)}, f32[256,256]{1,0:T(8,128)S(1)}) custom-call(bf16[1024,288]{1,0:T(8,128)(2,1)S(1)} %copy.11.refs_0_, bf16[32,1152]{1,0:T(8,128)(2,1)S(1)} %copy-done.3, bf16[1152,1024]{1,0:T(8,128)(2,1)S(1)} %copy-done, bf16[4,288,1024]{2,1,0:T(8,128)(2,1)} %bitcast.8, bf16[4,288,1024]{2,1,0:T(8,128)(2,1)} %bitcast.9), custom_call_target="tpu_custom_call" | custom-call | tf_op jit(solution)/shard_map/attend/pallas_call | solution.py:556
  67.4 0.0 copy-start.1
  67.4 0.8 copy-done.1
  68.2 0.0 copy-start.2
  68.2 0.7 copy-done.2
  68.9 95.6 %block.1 = bf16[2,2,16,1024]{3,2,1,0:T(8,128)(2,1)} custom-call(bf16[2,8,16,1024]{3,2,1,0:T(8,128)(2,1)} %bitcast.6, f32[2,8,16,256]{3,2,1,0:T(8,128)} %bitcast.7, f32[1,1024]{1,0:T(1,128)} %bitcast.11, bf16[1024,1024]{1,0:T(8,128)(2,1)} %refs_3_.1, bf16[1024,4096]{1,0:T(8,128)(2,1)} %refs_4_.1, bf16[1024,4096]{1,0:T(8,128)(2,1)} %refs_5_.1, ...), custom_call_target="tpu_custom_call" | custom-call | tf_op jit(solution)/shard_map/block/pallas_call | solution.py:583
  164.5 1.6 copy.13
Async XLA Ops:
  1.4 1.7 %copy-start = (bf16[1152,1024]{1,0:T(8,128)(2,1)S(1)}, bf16[1152,1024]{1,0:T(8,128)(2,1)}, u32[]{:S(2)}) copy-start(bf16[1152,1024]{1,0:T(8,128)(2,1)} %refs_2_.1) | copy-start | bytes 7077892
  3.1 0.9 copy-start.3
  67.4 0.8 copy-start.1
  68.2 0.7 copy-start.2

commit v3 on v2

--- a/solution.py
+++ b/solution.py
@@ -55,7 +55,7 @@
     hz = lax.axis_index("heads")
     width = wq.shape[1]
     heads = width // HDIM
-    tokens = fr.shape[0]
+    tokens = fr.shape[1]
 
     c_q = pltpu.make_async_copy(wq, wq_v, w_sem.at[0])
     c_k = pltpu.make_async_copy(wk, wkv.at[0], w_sem.at[1])
@@ -121,9 +121,10 @@
     def project(x, b, first):
         def tile(i):
             rows = pl.ds(pl.multiple_of(i * tt, tt), tt)
-            xb = x[rows, :]
+            xb = x[:, rows]
             for w in range(2):
-                term = jnp.dot(xb, wkv[w, b], preferred_element_type=F32)
+                term = lax.dot_general(xb, wkv[w, b], (((0,), (0,)), ((), ())),
+                                       preferred_element_type=F32)
                 if first:
                     acc[w, rows, :] = term
                 else:
@@ -562,7 +563,7 @@
             in_specs=[vmem, vmem, any_, any_, any_],
             out_specs=[vmem, vmem],
             scratch_shapes=[
-                pltpu.VMEM((nh, tokens, feats), BF16),
+                pltpu.VMEM((nh, feats, tokens), BF16),
                 pltpu.VMEM((nf, r, width), BF16),
                 pltpu.VMEM(w_query.shape, BF16),
                 pltpu.VMEM((2, nh, feats, width), BF16),
@@ -570,10 +571,10 @@
                 dma((3,)), dma((nh,)), dma((nh,)), dma((nh,)), dma((nf,)), dma((nf,)),
             ],
             compiler_params=pltpu.CompilerParams(
-                collective_id=0, has_side_effects=True, vmem_limit_bytes=48 * MIB),
+                collective_id=0, has_side_effects=True, vmem_limit_bytes=60 * MIB),
             name="attend",
         )(
-            frames, latents, w_query,
+            frames.T, latents, w_query,
             w_key.reshape(nh, feats, width), w_value.reshape(nh, feats, width),
         )
         cols_d = w_out.shape[1]

time: 166 us -> 150 us (0.904)
  Pallas kernels: 159 us -> 148 us
  local copies, waits for them, and re-layouts: 7.01 us -> 1.57 us
    pallas_call x1, Pallas kernels: 63.4 us -> 52.7 us  [on_device(): pl.pallas_call(lambda *refs: attend_kernel(nf, nh, ng, *refs), out_shape=...]
    unnamed x10 -> x1, local copies, waits for them, and re-layouts: 7.01 us -> 1.57 us
where the time goes in v3:
time: 150 us
  Pallas kernels  148 us (99%)
  local copies, waits for them, and re-layouts  1.57 us (1%)
    pallas_call x1, Pallas kernels, on_device(): pl.pallas_call(lambda *refs: block_kernel(nf, nh, ng, ny, nx, *refs), out...  95.6 us
    pallas_call x1, Pallas kernels, on_device(): pl.pallas_call(lambda *refs: attend_kernel(nf, nh, ng, *refs), out_shape=...  52.7 us

profile of v3, /device:TPU:24, one launch (start us, length us, event | category | flops | bytes accessed | tf_op | source)
XLA Modules:
  0.0 149.9 jit_solution(12505131499414492862)
XLA Ops:
  0.0 52.7 %attend.1 = (bf16[256,1024]{1,0:T(8,128)(2,1)}, f32[256,256]{1,0:T(8,128)}) custom-call(bf16[288,1024]{1,0:T(8,128)(2,1)} %bitcast.9, bf16[32,1152]{1,0:T(8,128)(2,1)} %refs_1_.1, bf16[1152,1024]{1,0:T(8,128)(2,1)} %refs_2_.1, bf16[4,288,1024]{2,1,0:T(8,128)(2,1)} %bitcast.7, bf16[4,288,1024]{2,1,0:T(8,128)(2,1)} %bitcast.8), custom_call_target="tpu_custom_call" | custom-call | tf_op jit(solution)/shard_map/attend/pallas_call | solution.py:557
  52.7 95.6 %block.1 = bf16[2,2,16,1024]{3,2,1,0:T(8,128)(2,1)} custom-call(bf16[2,8,16,1024]{3,2,1,0:T(8,128)(2,1)} %bitcast.10, f32[2,8,16,256]{3,2,1,0:T(8,128)} %bitcast.12, f32[1,1024]{1,0:T(1,128)} %bitcast.13, bf16[1024,1024]{1,0:T(8,128)(2,1)} %refs_3_.1, bf16[1024,4096]{1,0:T(8,128)(2,1)} %refs_4_.1, bf16[1024,4096]{1,0:T(8,128)(2,1)} %refs_5_.1, ...), custom_call_target="tpu_custom_call" | custom-call | tf_op jit(solution)/shard_map/block/pallas_call | solution.py:584
  148.4 1.6 %copy.12 = bf16[64,1024]{1,0:T(8,128)(2,1)} copy(bf16[64,1024]{1,0:T(8,128)(2,1)} %bitcast.11) | data formatting | bytes 262144
